TPU v7x, 32 devices: a whole 2x2x4 slice. The times are simulated.
32 devices in a mesh: groups: 2 (over y), inst: 4 (over x, core), tp: 4 (over z).
Axes of the slice: x: 2, y: 2, z: 4, core: 2. Of those that a mesh axis runs over, the one named last changes fastest.
Arguments:
- hidden: bfloat16 [2048, 5120], P(('groups', 'inst'), 'tp'), parts along dimension 0, may hold values from -6 to 6
- k_weight: bfloat16 [5120, 1024], P('inst', 'tp'), may hold values from -0.078125 to 0.078125
- v_weight: bfloat16 [5120, 1024], P('inst', 'tp'), may hold values from -0.078125 to 0.078125
- k_gain: float32 [128], replicated, may hold values from 0.25 to 1.75
- queries: bfloat16 [2048, 8192], P(('groups', 'inst'), 'tp'), parts along dimension 0, may hold values from -8 to 8
- kv_pool: bfloat16 [2, 432, 128, 1024], P(None, ('groups', 'inst'), None, 'tp'), parts along dimension 1, may hold values from -8 to 8
- page_holder: int32 [8, 48], P(('groups', 'inst')), parts along dimension 0, may hold values from 0 to 3, as said below
- page_slot: int32 [8, 48], P(('groups', 'inst')), parts along dimension 0, may hold values from 0 to 53, as said below
- page_count: int32 [8], P(('groups', 'inst')), parts along dimension 0, may hold values from 12 to 48, as said below
- write_owner: int32 [8, 2], P(('groups', 'inst')), parts along dimension 0, may hold values from 0 to 3, as said below
- write_slot: int32 [8, 2], P(('groups', 'inst')), parts along dimension 0, may hold values from 0 to 53, as said below
Outputs:
- attention_out: bfloat16 [2048, 8192], P(('groups', 'inst'), 'tp'), parts along dimension 0
- new_pool: bfloat16 [2, 432, 128, 1024], P(None, ('groups', 'inst'), None, 'tp'), parts along dimension 1
There are 2 independent parts, one for each index of `groups`. A program takes and returns all parts, laid end to end along the dimension named above; an argument that names none is the same for every part. Nothing has to cross between parts.
Inputs may be any that keep to these rules, and one draw needn't show every extreme that they name: `page_holder`: no request has more than 18 of its pages j < page_count on one instance; the request with 48 pages has exactly 18 on one instance. `page_slot`: the history pages in use and the new pages' slots are distinct slots of their instance. `page_count`: one request has exactly 48 pages. `write_owner`: the 2 new pages of one request go to distinct instances. `write_slot`: distinct from every slot in use on the same instance.
All inputs are finite; a program needn't handle non-finite values.
Results may differ from a plain program's by a relative error of at most 0.0039.
Values may be sent and summed in bfloat16 or wider, within the bound.
No kernel may reach another device: no remote copies, remote signals or barrier semaphores. Data moves between devices by JAX's collectives and lax.ppermute only.
A program may use at most 192 MiB of HBM per device.

v0:
```python
import math

import jax
import jax.numpy as jnp
from jax import lax
from jax.sharding import PartitionSpec as P

HD = 128
PAGE = 128
NEWP = 2
GROUP = 8


def normalize_rotate(raw_keys, k_gain, positions):
    per_head = raw_keys.reshape(raw_keys.shape[0], -1, HD)
    inverse_rms = lax.rsqrt(jnp.mean(per_head * per_head, axis=-1, keepdims=True) + 1e-06)
    per_head = per_head * inverse_rms * k_gain
    frequency = 1000000.0 ** (-(jnp.arange(HD // 2, dtype=jnp.float32) * 2.0) / HD)
    angles = positions.astype(jnp.float32)[:, None] * frequency[None, :]
    cosine = jnp.cos(angles)[:, None, :]
    sine_part = jnp.sin(angles)[:, None, :]
    first_half = per_head[..., : HD // 2]
    second = per_head[..., HD // 2 :]
    rotated = jnp.concatenate(
        [first_half * cosine - second * sine_part, second * cosine + first_half * sine_part],
        axis=-1,
    )
    return rotated.reshape(raw_keys.shape)


def requested(holder_row, slot_row, page_total, inst_count, capacity):
    pages_listed = holder_row.shape[0]
    live_pages = jnp.arange(pages_listed, dtype=jnp.int32) < page_total
    on_holder = (
        holder_row[:, None] == jnp.arange(inst_count, dtype=jnp.int32)[None, :]
    ) & live_pages[:, None]
    page_rank = jnp.cumsum(on_holder.astype(jnp.int32), axis=0) - 1
    own_rank = jnp.sum(jnp.where(on_holder, page_rank, 0), axis=1)
    target = jnp.where(live_pages, holder_row * capacity + own_rank, -1)
    chosen = jnp.arange(inst_count * capacity, dtype=jnp.int32)[:, None] == target[None, :]
    slot_list = jnp.sum(jnp.where(chosen, slot_row[None, :], 0), axis=1).reshape(
        inst_count, capacity
    )
    valid = jnp.any(chosen, axis=1).reshape(inst_count, capacity)
    return (slot_list, valid)


def per_device(
    hidden,
    k_weight,
    v_weight,
    k_gain,
    queries,
    kv_pool,
    page_holder,
    page_slot,
    page_count,
    write_owner,
    write_slot,
):
    inst_count = lax.axis_size("inst")
    own_index = lax.axis_index("inst")
    capacity = 3 * page_holder.shape[1] // (2 * inst_count)
    features = lax.all_gather(hidden, "tp", axis=1, tiled=True)
    new_count = features.shape[0]
    local_width = k_weight.shape[1]
    kv_local = local_width // HD
    raw_keys = jnp.dot(
        features,
        lax.all_gather(k_weight, "inst", axis=0, tiled=True),
        preferred_element_type=jnp.float32,
    )
    raw_values = jnp.dot(
        features,
        lax.all_gather(v_weight, "inst", axis=0, tiled=True),
        preferred_element_type=jnp.float32,
    )
    positions = page_count[0] * PAGE + jnp.arange(new_count, dtype=jnp.int32)
    new_keys = normalize_rotate(raw_keys, k_gain, positions).astype(jnp.bfloat16)
    new_values = raw_values.astype(jnp.bfloat16)
    own_slots, own_valid = requested(
        page_holder[0], page_slot[0], page_count[0], inst_count, capacity
    )
    served = lax.all_to_all(own_slots, "inst", split_axis=0, concat_axis=0, tiled=True)
    served_pages = kv_pool[:, served.reshape(-1)].reshape(
        2, inst_count, capacity, PAGE, local_width
    )
    fetched = lax.all_to_all(served_pages, "inst", split_axis=1, concat_axis=1, tiled=True)
    scale_root = math.sqrt(HD)
    query_heads = queries.reshape(new_count, kv_local, GROUP, HD)
    key_heads = new_keys.reshape(new_count, kv_local, HD)
    value_heads = new_values.reshape(new_count, kv_local, HD)
    scores = (
        jnp.einsum("qkgd,skd->kgqs", query_heads, key_heads, preferred_element_type=jnp.float32)
        / scale_root
    )
    causal = jnp.arange(new_count)[None, :] <= jnp.arange(new_count)[:, None]
    scores = jnp.where(causal, scores, -jnp.inf)
    row_max = jnp.max(scores, axis=-1, keepdims=True)
    probabilities = jnp.exp(scores - row_max)
    totals = jnp.sum(probabilities, axis=-1, keepdims=True)
    numerator = jnp.einsum(
        "kgqs,skd->kgqd",
        probabilities.astype(jnp.bfloat16),
        value_heads,
        preferred_element_type=jnp.float32,
    )

    def absorb(running, block_data):
        running_max, running_totals, running_numerator = running
        block_keys, block_values, block_valid = block_data
        block_keys = block_keys.reshape(capacity * PAGE, kv_local, HD)
        block_values = block_values.reshape(capacity * PAGE, kv_local, HD)
        block_scores = (
            jnp.einsum(
                "qkgd,skd->kgqs", query_heads, block_keys, preferred_element_type=jnp.float32
            )
            / scale_root
        )
        allowed = jnp.repeat(block_valid, PAGE)
        block_scores = jnp.where(allowed, block_scores, -jnp.inf)
        new_max = jnp.maximum(running_max, jnp.max(block_scores, axis=-1, keepdims=True))
        rescale = jnp.exp(running_max - new_max)
        block_probs = jnp.exp(block_scores - new_max)
        running_totals = running_totals * rescale + jnp.sum(block_probs, axis=-1, keepdims=True)
        running_numerator = running_numerator * rescale + jnp.einsum(
            "kgqs,skd->kgqd",
            block_probs.astype(jnp.bfloat16),
            block_values,
            preferred_element_type=jnp.float32,
        )
        return ((new_max, running_totals, running_numerator), None)

    final_state, leftover = lax.scan(
        absorb, (row_max, totals, numerator), (fetched[0], fetched[1], own_valid)
    )
    attention = final_state[2] / final_state[1]
    attention_out = (
        attention.transpose(2, 0, 1, 3)
        .reshape(new_count, kv_local * GROUP * HD)
        .astype(jnp.bfloat16)
    )
    stacked = jnp.stack(
        [new_keys.reshape(NEWP, PAGE, local_width), new_values.reshape(NEWP, PAGE, local_width)],
        axis=1,
    )
    slot_range = jnp.arange(kv_pool.shape[1], dtype=jnp.int32)
    arrived, owners, slot_list = (
        lax.all_gather(stacked, "inst", axis=0, tiled=True),
        lax.all_gather(write_owner[0], "inst", axis=0, tiled=True),
        lax.all_gather(write_slot[0], "inst", axis=0, tiled=True),
    )
    matches = (owners[None, :] == own_index) & (slot_list[None, :] == slot_range[:, None])
    written = jnp.any(matches, axis=1)
    placed = jnp.einsum(
        "sk,kxpc->xspc", matches.astype(jnp.bfloat16), arrived, preferred_element_type=jnp.float32
    ).astype(jnp.bfloat16)
    new_pool = jnp.where(written[None, :, None, None], placed, kv_pool)
    return (attention_out, new_pool)


def solution(mesh):
    return jax.shard_map(
        per_device,
        mesh=mesh,
        in_specs=(
            P(("groups", "inst"), "tp"),
            P("inst", "tp"),
            P("inst", "tp"),
            P(),
            P(("groups", "inst"), "tp"),
            P(None, ("groups", "inst"), None, "tp"),
            P(("groups", "inst"), None),
            P(("groups", "inst"), None),
            P(("groups", "inst")),
            P(("groups", "inst"), None),
            P(("groups", "inst"), None),
        ),
        out_specs=(P(("groups", "inst"), "tp"), P(None, ("groups", "inst"), None, "tp")),
        check_vma=False,
    )
```

profile of v0, /device:TPU:5, one launch (start us, length us, event | category | flops | bytes accessed | tf_op | source)
XLA Modules:
  0.0 461.7 jit_solution(8664570618433025245)
XLA Ops:
  12.5 6.3 %all_to_all.14 = s32[4,1,18]{2,1,0:T(1,128)S(1)} all-to-all(s32[4,1,18]{2,1,0:T(1,128)S(1)} %bitcast.138), channel_id=1, replica_groups=mesh['groups'=2,'inst'=4,'tp'=4] {'inst'}, dimensions={0} | all-to-all | bytes 576 | tf_op jit(solution)/shard_map/all_to_all | solution.py:84
  20.0 9.0 %gather_fusion = bf16[72,2,128,256]{3,2,1,0:T(8,128)(2,1)} fusion(bf16[2,54,128,256]{3,2,1,0:T(8,128)(2,1)} %param.18, s32[1024]{0:T(1024)S(1)} %pad_clamp_fusion), kind=kCustom, calls=%fused_computation | custom fusion | bytes 18874656 | tf_op jit(solution)/shard_map/gather | solution.py:85
  29.1 8.8 %copy.99 = bf16[2,4,18,128,256]{4,3,2,0,1:T(8,128)(2,1)} copy(bf16[2,4,18,128,256]{4,3,0,2,1:T(8,128)(2,1)} %bitcast.124) | data formatting | bytes 18874368 | tf_op jit(solution)/shard_map/reshape | solution.py:85
  37.8 6.5 %all-to-all-start.1 = ((bf16[2,4,18,128,256]{4,3,2,0,1:T(8,128)(2,1)}), bf16[2,4,18,128,256]{4,3,2,0,1:T(8,128)(2,1)}, u32[]{:S(2)}, u32[]{:S(2)}) async-start(bf16[2,4,18,128,256]{4,3,2,0,1:T(8,128)(2,1)} %copy.99), calls=%async_computation.1 | async-start | bytes 18874368 | tf_op jit(solution)/shard_map/all_to_all | solution.py:88
  46.6 129.5 %all-reduce.2 = (s32[8]{0:T(128)S(1)}, s32[8]{0:T(128)S(1)}) all-reduce(s32[8]{0:T(128)S(1)} %bitcast_dynamic-update-slice_fusion, s32[8]{0:T(128)S(1)} %bitcast_dynamic-update-slice_fusion.1), channel_id=3, replica_groups=mesh['groups'=2,'inst'=4,'tp'=4] {'inst'}, use_global_device_ids=true, to_apply=%add.1 | all-reduce | flops 16 | bytes 128
  177.4 1.3 copy.100
  179.3 3.7 multiply_reduce_fusion
  183.8 3.4 convolution_convert_fusion
  188.9 1.5 fusion.15
  190.3 2.6 fusion.17
  192.9 12.7 %all-gather.13.cloned.1.call-done = bf16[8,2,128,256]{3,2,1,0:T(8,128)(2,1)} async-done(((bf16[2,2,128,256]{3,2,1,0:T(8,128)(2,1)}), bf16[8,2,128,256]{3,2,1,0:T(8,128)(2,1)}) %all-gather.13.cloned.1.call-update) | async-done | bytes 1048592 | tf_op jit(solution)/shard_map/all_gather | solution.py:149
  205.7 9.7 %bitcast_select_fusion = bf16[2,54,128,256]{3,1,2,0:T(8,128)(2,1)S(1)} fusion(bf16[2,54,128,256]{3,2,1,0:T(8,128)(2,1)} %param.18, pred[54]{0:T(512)(128)(4,1)S(1)} %fusion.33, bf16[8,2,128,256]{3,2,1,0:T(8,128)(2,1)} %all-gather.13.cloned.1.call-done, s32[8]{0:T(128)S(1)} %get-tuple-element.115, pred[8]{0:T(512)(128)(4,1)S(1)} %broadcast_compare_fusion), kind=kOutput, calls=%fused_computation.23 | convolution fusion | flops 63701856 | bytes 15204446 | tf_op jit(solution)/shard_map/sk,kxpc->xspc/dot_general | solution.py:155
  215.3 4.9 %copy.106 = bf16[2,54,128,256]{3,2,1,0:T(8,128)(2,1)} copy(bf16[2,54,128,256]{3,1,2,0:T(8,128)(2,1)S(1)} %bitcast_select_fusion) | data formatting | bytes 14155776
  220.3 8.8 %slice_bitcast_fusion = (bf16[4,18,128,256]{3,2,1,0:T(8,128)(2,1)}, bf16[4,18,128,256]{3,2,1,0:T(8,128)(2,1)}) fusion(bf16[2,4,18,128,256]{4,3,2,0,1:T(8,128)(2,1)} %all-to-all-done.1), kind=kLoop, calls=%fused_computation.24 | loop fusion | bytes 18874368 | tf_op jit(solution)/shard_map/squeeze | solution.py:135
  229.0 222.3 %while.14 = (s32[]{:T(128)}, f32[2,8,256,1]{2,1,0,3:T(8,128)S(1)}, f32[2,8,256,1]{2,1,0,3:T(8,128)}, f32[2,8,256,128]{3,2,1,0:T(8,128)}, pred[4,18]{1,0:T(4,128)...) while((s32[]{:T(128)}, f32[2,8,256,1]{2,1,0,3:T(8,128)S(1)}, ...), condition=%wide.region_10.11_spmd, body=%wide.region_7.10_spmd.sunk | while | flops 4936708096 | bytes 130688216 | solution.py:134
  229.0 1.8 constant_dynamic-slice_fusion.3
  231.9 15.6 %bitcast_reduce_fusion.2 = (f32[2,8,256]{2,1,0:T(8,128)S(1)}, f32[2,2304,256,8]{2,1,3,0:T(8,128)}) fusion(pred[2304]{0:T(1024)(128)(4,1)S(1)} %broadcast_bitcast_fusion.2, bf16[256,2,8,128]{3,0,2,1:T(8,128)(2,1)} %get-tuple-element.218, bf16[2304,2,128,1]{2,1,0,3:T(2,128)(2,1)S(1)} %bitcast.123), kind=kOutput, calls=%fused_computation.2.clone.1 | convolution fusion | flops 2444226560 | bytes 39995648 | tf_op jit(solution)/shard_map/while/body/eval_jaxpr/qkgd,skd->kgqs/dot_general | solution.py:115
  247.8 19.9 %multiply_add_fusion.3 = f32[2,8,256,128]{3,2,1,0:T(8,128)} fusion(f32[2,8,256,128]{3,2,1,0:T(8,128)} %get-tuple-element.206, f32[2,2304,256,8]{2,1,3,0:T(8,128)} %get-tuple-element.191, f32[2,8,256]{2,1,0:T(8,128)S(1)} %bitcast.128, pred[2304]{0:T(1024)(128)(4,1)S(1)} %broadcast_bitcast_fusion.2, bf16[2304,2,128,1]{2,1,0,3:T(2,128)(2,1)S(1)} %bitcast.125, ...), kind=kOutput, calls=%fused_computation.9.clone.1 | convolution fusion | flops 2454716416 | bytes 43157760 | tf_op jit(solution)/shard_map/while/body/eval_jaxpr/kgqs,skd->kgqd/dot_general | solution.py:126
  267.7 16.3 %fusion.56 = f32[2,8,256]{2,1,0:T(8,128)S(1)} fusion(f32[2,2304,256,8]{2,1,3,0:T(8,128)} %get-tuple-element.191, f32[2,8,256]{2,1,0:T(8,128)S(1)} %bitcast.129, pred[2304]{0:T(1024)(128)(4,1)S(1)} %broadcast_bitcast_fusion.2), kind=kLoop, calls=%fused_computation.6.clone.1 | loop fusion | flops 37744640 | bytes 37783808 | tf_op jit(solution)/shard_map/while/body/eval_jaxpr/reduce_sum | solution.py:125
  284.6 1.8 constant_dynamic-slice_fusion.3
  287.5 15.6 %bitcast_reduce_fusion.2 = (f32[2,8,256]{2,1,0:T(8,128)S(1)}, f32[2,2304,256,8]{2,1,3,0:T(8,128)}) fusion(pred[2304]{0:T(1024)(128)(4,1)S(1)} %broadcast_bitcast_fusion.2, bf16[256,2,8,128]{3,0,2,1:T(8,128)(2,1)} %get-tuple-element.218, bf16[2304,2,128,1]{2,1,0,3:T(2,128)(2,1)S(1)} %bitcast.123), kind=kOutput, calls=%fused_computation.2.clone.1 | convolution fusion | flops 2444226560 | bytes 39995648 | tf_op jit(solution)/shard_map/while/body/eval_jaxpr/qkgd,skd->kgqs/dot_general | solution.py:115
  303.4 19.9 %multiply_add_fusion.3 = f32[2,8,256,128]{3,2,1,0:T(8,128)} fusion(f32[2,8,256,128]{3,2,1,0:T(8,128)} %get-tuple-element.206, f32[2,2304,256,8]{2,1,3,0:T(8,128)} %get-tuple-element.191, f32[2,8,256]{2,1,0:T(8,128)S(1)} %bitcast.128, pred[2304]{0:T(1024)(128)(4,1)S(1)} %broadcast_bitcast_fusion.2, bf16[2304,2,128,1]{2,1,0,3:T(2,128)(2,1)S(1)} %bitcast.125, ...), kind=kOutput, calls=%fused_computation.9.clone.1 | convolution fusion | flops 2454716416 | bytes 43157760 | tf_op jit(solution)/shard_map/while/body/eval_jaxpr/kgqs,skd->kgqd/dot_general | solution.py:126
  323.2 16.3 %fusion.56 = f32[2,8,256]{2,1,0:T(8,128)S(1)} fusion(f32[2,2304,256,8]{2,1,3,0:T(8,128)} %get-tuple-element.191, f32[2,8,256]{2,1,0:T(8,128)S(1)} %bitcast.129, pred[2304]{0:T(1024)(128)(4,1)S(1)} %broadcast_bitcast_fusion.2), kind=kLoop, calls=%fused_computation.6.clone.1 | loop fusion | flops 37744640 | bytes 37783808 | tf_op jit(solution)/shard_map/while/body/eval_jaxpr/reduce_sum | solution.py:125
  340.2 1.8 constant_dynamic-slice_fusion.3
  343.0 15.6 %bitcast_reduce_fusion.2 = (f32[2,8,256]{2,1,0:T(8,128)S(1)}, f32[2,2304,256,8]{2,1,3,0:T(8,128)}) fusion(pred[2304]{0:T(1024)(128)(4,1)S(1)} %broadcast_bitcast_fusion.2, bf16[256,2,8,128]{3,0,2,1:T(8,128)(2,1)} %get-tuple-element.218, bf16[2304,2,128,1]{2,1,0,3:T(2,128)(2,1)S(1)} %bitcast.123), kind=kOutput, calls=%fused_computation.2.clone.1 | convolution fusion | flops 2444226560 | bytes 39995648 | tf_op jit(solution)/shard_map/while/body/eval_jaxpr/qkgd,skd->kgqs/dot_general | solution.py:115
  358.9 19.9 %multiply_add_fusion.3 = f32[2,8,256,128]{3,2,1,0:T(8,128)} fusion(f32[2,8,256,128]{3,2,1,0:T(8,128)} %get-tuple-element.206, f32[2,2304,256,8]{2,1,3,0:T(8,128)} %get-tuple-element.191, f32[2,8,256]{2,1,0:T(8,128)S(1)} %bitcast.128, pred[2304]{0:T(1024)(128)(4,1)S(1)} %broadcast_bitcast_fusion.2, bf16[2304,2,128,1]{2,1,0,3:T(2,128)(2,1)S(1)} %bitcast.125, ...), kind=kOutput, calls=%fused_computation.9.clone.1 | convolution fusion | flops 2454716416 | bytes 43157760 | tf_op jit(solution)/shard_map/while/body/eval_jaxpr/kgqs,skd->kgqd/dot_general | solution.py:126
  378.8 16.3 %fusion.56 = f32[2,8,256]{2,1,0:T(8,128)S(1)} fusion(f32[2,2304,256,8]{2,1,3,0:T(8,128)} %get-tuple-element.191, f32[2,8,256]{2,1,0:T(8,128)S(1)} %bitcast.129, pred[2304]{0:T(1024)(128)(4,1)S(1)} %broadcast_bitcast_fusion.2), kind=kLoop, calls=%fused_computation.6.clone.1 | loop fusion | flops 37744640 | bytes 37783808 | tf_op jit(solution)/shard_map/while/body/eval_jaxpr/reduce_sum | solution.py:125
  395.7 1.8 constant_dynamic-slice_fusion.3
  398.6 15.6 %bitcast_reduce_fusion.2 = (f32[2,8,256]{2,1,0:T(8,128)S(1)}, f32[2,2304,256,8]{2,1,3,0:T(8,128)}) fusion(pred[2304]{0:T(1024)(128)(4,1)S(1)} %broadcast_bitcast_fusion.2, bf16[256,2,8,128]{3,0,2,1:T(8,128)(2,1)} %get-tuple-element.218, bf16[2304,2,128,1]{2,1,0,3:T(2,128)(2,1)S(1)} %bitcast.123), kind=kOutput, calls=%fused_computation.2.clone.1 | convolution fusion | flops 2444226560 | bytes 39995648 | tf_op jit(solution)/shard_map/while/body/eval_jaxpr/qkgd,skd->kgqs/dot_general | solution.py:115
  414.5 19.9 %multiply_add_fusion.3 = f32[2,8,256,128]{3,2,1,0:T(8,128)} fusion(f32[2,8,256,128]{3,2,1,0:T(8,128)} %get-tuple-element.206, f32[2,2304,256,8]{2,1,3,0:T(8,128)} %get-tuple-element.191, f32[2,8,256]{2,1,0:T(8,128)S(1)} %bitcast.128, pred[2304]{0:T(1024)(128)(4,1)S(1)} %broadcast_bitcast_fusion.2, bf16[2304,2,128,1]{2,1,0,3:T(2,128)(2,1)S(1)} %bitcast.125, ...), kind=kOutput, calls=%fused_computation.9.clone.1 | convolution fusion | flops 2454716416 | bytes 43157760 | tf_op jit(solution)/shard_map/while/body/eval_jaxpr/kgqs,skd->kgqd/dot_general | solution.py:126
  434.4 16.3 %fusion.56 = f32[2,8,256]{2,1,0:T(8,128)S(1)} fusion(f32[2,2304,256,8]{2,1,3,0:T(8,128)} %get-tuple-element.191, f32[2,8,256]{2,1,0:T(8,128)S(1)} %bitcast.129, pred[2304]{0:T(1024)(128)(4,1)S(1)} %broadcast_bitcast_fusion.2), kind=kLoop, calls=%fused_computation.6.clone.1 | loop fusion | flops 37744640 | bytes 37783808 | tf_op jit(solution)/shard_map/while/body/eval_jaxpr/reduce_sum | solution.py:125
  451.3 2.0 fusion.24
  (105 shorter events, 21.6 us)
Async XLA Ops:
  7.2 172.1 %all-gather.7.cloned.1.call-start = ((), (), s32[]{:S(2)}) async-start(), calls=%async_computation.2 | async-start | bytes 3276800 | tf_op jit(solution)/shard_map/all_gather | solution.py:64
  7.9 171.4 %all-gather.9.cloned.1.call-start = ((), (), s32[]{:S(2)}) async-start(), calls=%async_computation.3 | async-start | bytes 3276800 | tf_op jit(solution)/shard_map/all_gather | solution.py:70
  37.8 7.3 %copy-start.6 = (u32[32]{0:T(128)S(1)}, u32[32]{0:T(128)}, u32[]{:S(2)}) copy-start(u32[32]{0:T(128)} %constant.66) | copy-start | bytes 388
  37.8 8.5 %copy-start.4 = (s32[1,2]{1,0:T(1,128)S(1)}, s32[1,2]{1,0:T(1,128)}, u32[]{:S(2)}) copy-start(s32[1,2]{1,0:T(1,128)} %param.23) | copy-start | bytes 28
  37.8 8.6 %copy-start.5 = (s32[1,2]{1,0:T(1,128)S(1)}, s32[1,2]{1,0:T(1,128)}, u32[]{:S(2)}) copy-start(s32[1,2]{1,0:T(1,128)} %param.22) | copy-start | bytes 28
  37.8 138.3 %copy-start = (bf16[256,2048]{1,0:T(8,128)(2,1)S(1)}, bf16[256,2048]{1,0:T(8,128)(2,1)}, u32[]{:S(2)}) copy-start(bf16[256,2048]{1,0:T(8,128)(2,1)} %param.17) | copy-start | bytes 3145732
  37.8 182.4 %all-to-all-start.1 = ((bf16[2,4,18,128,256]{4,3,2,0,1:T(8,128)(2,1)}), bf16[2,4,18,128,256]{4,3,2,0,1:T(8,128)(2,1)}, u32[]{:S(2)}, u32[]{:S(2)}) async-start(bf16[2,4,18,128,256]{4,3,2,0,1:T(8,128)(2,1)} %copy.99), calls=%async_computation.1 | async-start | bytes 18874368 | tf_op jit(solution)/shard_map/all_to_all | solution.py:88
  44.3 139.5 %all-gather.11.cloned.1.call-start = ((), (), s32[]{:S(2)}) async-start(), calls=%async_computation.4 | async-start | bytes 3276800 | tf_op jit(solution)/shard_map/all_gather | solution.py:75
  45.0 160.6 %all-gather.13.cloned.1.call-start = ((), (), s32[]{:S(2)}) async-start(), calls=%async_computation.5 | async-start | bytes 1310720 | tf_op jit(solution)/shard_map/all_gather | solution.py:149
  177.4 5.7 %copy-start.3 = (f32[128]{0:T(128)S(1)}, f32[128]{0:T(128)}, u32[]{:S(2)}) copy-start(f32[128]{0:T(128)} %param.16) | copy-start | bytes 1540
  267.7 16.3 %copy-start.1 = (f32[2,8,256,1]{2,1,0,3:T(8,128)S(1)}, f32[2,8,256,1]{2,1,0,3:T(8,128)}, u32[]{:S(2)}) copy-start(f32[2,8,256,1]{2,1,0,3:T(8,128)} %get-tuple-element.205) | copy-start | bytes 49156 | tf_op jit(solution)/shard_map/while
  284.0 0.6 copy-start.2
  323.2 16.3 %copy-start.1 = (f32[2,8,256,1]{2,1,0,3:T(8,128)S(1)}, f32[2,8,256,1]{2,1,0,3:T(8,128)}, u32[]{:S(2)}) copy-start(f32[2,8,256,1]{2,1,0,3:T(8,128)} %get-tuple-element.205) | copy-start | bytes 49156 | tf_op jit(solution)/shard_map/while
  339.6 0.6 copy-start.2
  378.8 16.3 %copy-start.1 = (f32[2,8,256,1]{2,1,0,3:T(8,128)S(1)}, f32[2,8,256,1]{2,1,0,3:T(8,128)}, u32[]{:S(2)}) copy-start(f32[2,8,256,1]{2,1,0,3:T(8,128)} %get-tuple-element.205) | copy-start | bytes 49156 | tf_op jit(solution)/shard_map/while
  395.1 0.6 copy-start.2
  434.4 16.3 %copy-start.1 = (f32[2,8,256,1]{2,1,0,3:T(8,128)S(1)}, f32[2,8,256,1]{2,1,0,3:T(8,128)}, u32[]{:S(2)}) copy-start(f32[2,8,256,1]{2,1,0,3:T(8,128)} %get-tuple-element.205) | copy-start | bytes 49156 | tf_op jit(solution)/shard_map/while
  450.7 0.6 copy-start.2
Sparse Core Ops, SparseCore 0:
  9.6 55.9 all-gather.6
  67.1 38.9 all-gather.8
  107.7 39.7 all-gather.10
  188.1 17.5 all-gather.12
where the time goes:
time: 464 us; the launch traced here: 462 us
  matrix products  162 us (35%)
  blocking collectives  136 us (29%)
  other arithmetic  73.6 us (16%)
  local copies, waits for them, and re-layouts  53.5 us (12%)
  between operations  15.3 us (3%)
  waiting for transfers between devices  14.9 us (3%)
  starting transfers between devices  6.59 us (1%)
    unnamed x1, blocking collectives  130 us
    dot_general x4, matrix products, absorb(): jnp.einsum('kgqs,skd->kgqd', block_probs.astype(jnp.bfloat16), block_valu...  79.5 us
    reduce_sum x4, other arithmetic, absorb(): jnp.sum(block_probs, axis=-1, keepdims=True)  65.2 us
    dot_general x4, matrix products, absorb(): jnp.einsum('qkgd,skd->kgqs', query_heads, block_keys, preferred_element_t...  62.3 us
    all_gather x1, waiting for transfers between devices, per_device(): lax.all_gather(stacked, 'inst', axis=0, tiled=True)  12.7 us
    dot_general x1, matrix products, per_device(): jnp.einsum('sk,kxpc->xspc', matches.astype(jnp.bfloat16), arrived, prefer...  9.67 us
  transfers between devices with their start and end apart: 5, of which 1 were waited for; matrix products, arithmetic and copies ran while one was open for 12% of the time, Pallas kernels for 0%

commit v1 on v0

v1 whole, which is shorter than its diff:
```python
import functools
import math

import jax
import jax.numpy as jnp
from jax import lax
from jax.experimental import pallas as pl
from jax.experimental.pallas import tpu as pltpu
from jax.sharding import PartitionSpec as P

HD = 128
PAGE = 128
GROUP = 8
BLOCK = GROUP * HD
EXTRA = 128
TABLE_ROWS = 16
EMPTY = -1e30
LOG2E = 1.4426950408889634
SCALE = LOG2E / math.sqrt(HD)
CHUNK = 4
ANY = pl.BlockSpec(memory_space=pl.ANY)
SMEM = pl.BlockSpec(memory_space=pltpu.SMEM)
VMEM_LIMIT = 56 * 1024 * 1024


def row_dot(a, b):
    return lax.dot_general(a, b, (((1,), (1,)), ((), ())), preferred_element_type=jnp.float32)


def plain_dot(a, b):
    return lax.dot_general(a, b, (((1,), (0,)), ((), ())), preferred_element_type=jnp.float32)


def split_stats(stat, head, lanes):
    high = stat.astype(jnp.bfloat16).astype(jnp.float32)
    rest = stat - high
    middle = rest.astype(jnp.bfloat16).astype(jnp.float32)
    low = rest - middle
    zero = jnp.zeros(lanes.shape, jnp.float32)
    terms = jnp.where(lanes == 3 * head, high, zero)
    terms = jnp.where(lanes == 3 * head + 1, middle, terms)
    return jnp.where(lanes == 3 * head + 2, low, terms)


def joined_stats(payload, head):
    term = lax.broadcasted_iota(jnp.int32, (EXTRA, HD), 0)
    picked = jnp.where((term >= 3 * head) & (term < 3 * head + 3), 1.0, 0.0).astype(jnp.bfloat16)
    return plain_dot(payload[:, BLOCK : BLOCK + EXTRA], picked)


def attend_kernel(
    pages_listed, capacity, requests, kv_heads, copy_pool, me_ref, table_ref, *refs
):
    items = requests * len(kv_heads)
    q_refs = refs[:items]
    pool_ref, out_ref = refs[items], refs[items + 1]
    rest = refs[items + 2 :]
    if copy_pool:
        new_pool_ref, rest = rest[0], rest[1:]
    q_buf, kv_buf, acc, maxima, totals, out_buf, slots, q_sem, kv_sem, out_sem, pool_sem = rest
    width = len(kv_heads)
    new_count = q_buf.shape[2]

    def q_copies(item):
        source, offset = q_refs[item]
        return [
            pltpu.make_async_copy(
                source.at[pl.ds(0, new_count), pl.ds(offset + head * HD, HD)],
                q_buf.at[item, head],
                q_sem.at[item, head],
            )
            for head in range(GROUP)
        ]

    def page_copy(request, place, slot):
        return [
            pltpu.make_async_copy(
                pool_ref.at[:, slot, :, pl.ds(kv_head * HD, HD)],
                kv_buf.at[request, column, :, place],
                kv_sem.at[request, column, place],
            )
            for column, kv_head in enumerate(kv_heads)
        ]

    me = me_ref[0]
    for request in range(requests):

        def look(page, found, request=request):
            mine = (page < table_ref[request, 2 * pages_listed]) & (table_ref[request, page] == me)

            @pl.when(mine)
            def _():
                for copy in page_copy(request, found, table_ref[request, pages_listed + page]):
                    copy.start()

            return found + mine.astype(jnp.int32)

        slots[request] = lax.fori_loop(0, pages_listed, look, 0)
    for item in range(items):
        for copy in q_copies(item):
            copy.start()
    pool_copies = []
    if copy_pool:
        slot_total = pool_ref.shape[1]
        parts = 6 if slot_total % 6 == 0 else 1
        step = slot_total // parts
        pool_copies = [
            pltpu.make_async_copy(
                pool_ref.at[index, pl.ds(part * step, step)],
                new_pool_ref.at[index, pl.ds(part * step, step)],
                pool_sem.at[index, part],
            )
            for index in range(2)
            for part in range(parts)
        ]
        for copy in pool_copies:
            copy.start()
    for item in range(items):
        for copy in q_copies(item):
            copy.wait()

    lanes = lax.broadcasted_iota(jnp.int32, (new_count, EXTRA), 1)

    def one_item(item, carry):
        request = item // width
        column = item % width
        found = slots[request]

        @pl.when(column == 0)
        def _():
            def arrived(place, carry):
                for copy in page_copy(request, place, 0):
                    copy.wait()
                return carry

            lax.fori_loop(0, found, arrived, 0)

        acc[...] = jnp.zeros(acc.shape, jnp.float32)
        totals[...] = jnp.zeros(totals.shape, jnp.float32)
        maxima[...] = jnp.full(maxima.shape, EMPTY, jnp.float32)

        def chunk(first, count):
            keys = kv_buf[request, column, 0, pl.ds(first, count)].reshape(count * PAGE, HD)
            values = kv_buf[request, column, 1, pl.ds(first, count)].reshape(count * PAGE, HD)
            for head in range(GROUP):
                scores = row_dot(q_buf[item, head], keys)
                old = maxima[head]
                top = jnp.maximum(old, jnp.max(scores, axis=1, keepdims=True) * SCALE)
                rescale = jnp.exp2(old - top)
                total = totals[head] * rescale
                parts = []
                for part in range(count):
                    piece = jnp.exp2(scores[:, part * PAGE : (part + 1) * PAGE] * SCALE - top)
                    total = total + piece
                    parts.append(piece.astype(jnp.bfloat16))
                weights = jnp.concatenate(parts, axis=1) if count > 1 else parts[0]
                maxima[head] = top
                totals[head] = total
                acc[head] = acc[head] * rescale + plain_dot(weights, values)

        whole = found // CHUNK
        left = found % CHUNK

        def step(index, carry):
            chunk(index * CHUNK, CHUNK)
            return carry

        lax.fori_loop(0, whole, step, 0)
        for count in range(1, CHUNK):

            @pl.when(left == count)
            def _(count=count):
                chunk(whole * CHUNK, count)

        def finish(head, terms):
            total = jnp.sum(totals[head], axis=1, keepdims=True)
            some = total > 0.0
            inverse = jnp.where(some, 1.0 / jnp.where(some, total, 1.0), 0.0)
            out_buf[item, head] = (acc[head] * inverse).astype(jnp.bfloat16)
            stat = jnp.where(
                some, maxima[head] + jnp.log2(jnp.where(some, total, 1.0)), EMPTY
            )
            return terms + split_stats(stat, head, lanes)

        terms = lax.fori_loop(
            0, GROUP, finish, jnp.zeros((new_count, EXTRA), jnp.float32)
        )
        out_buf[item, GROUP] = terms.astype(jnp.bfloat16)
        for copy in out_copies(item):
            copy.start()
        return carry

    def out_copies(item):
        return [
            pltpu.make_async_copy(
                out_buf.at[item, head],
                out_ref.at[item, :, pl.ds(head * HD, HD)],
                out_sem.at[item, head],
            )
            for head in range(GROUP + 1)
        ]

    lax.fori_loop(0, items, one_item, 0)
    for item in range(items):
        for copy in out_copies(item):
            copy.wait()
    for copy in pool_copies:
        copy.wait()


def attend(me, tables, q_items, kv_heads, pool, pages_listed, capacity, new_count, copy_pool=False):
    requests, width = tables.shape[0], len(kv_heads)
    items = requests * width
    out_shape = [jax.ShapeDtypeStruct((items, new_count, BLOCK + EXTRA), jnp.bfloat16)]
    out_specs = [ANY]
    if copy_pool:
        out_shape.append(jax.ShapeDtypeStruct(pool.shape, pool.dtype))
        out_specs.append(ANY)
    offsets = [offset for _, offset in q_items]

    def kernel(me_ref, table_ref, *refs):
        paired = [(ref, offset) for ref, offset in zip(refs[:items], offsets)]
        attend_kernel(
            pages_listed, capacity, requests, kv_heads, copy_pool, me_ref, table_ref,
            *paired, *refs[items:],
        )

    assumed = items * 8 * PAGE * GROUP * new_count
    result = pl.pallas_call(
        kernel,
        out_shape=out_shape,
        in_specs=[SMEM, SMEM] + [ANY] * (items + 1),
        out_specs=out_specs,
        scratch_shapes=[
            pltpu.VMEM((items, GROUP, new_count, HD), jnp.bfloat16),
            pltpu.VMEM((requests, width, 2, capacity, PAGE, HD), jnp.bfloat16),
            pltpu.VMEM((GROUP, new_count, HD), jnp.float32),
            pltpu.VMEM((GROUP, new_count, HD), jnp.float32),
            pltpu.VMEM((GROUP, new_count, HD), jnp.float32),
            pltpu.VMEM((items, GROUP + 1, new_count, HD), jnp.bfloat16),
            pltpu.SMEM((requests,), jnp.int32),
            pltpu.SemaphoreType.DMA((items, GROUP)),
            pltpu.SemaphoreType.DMA((requests, width, capacity)),
            pltpu.SemaphoreType.DMA((items, GROUP + 1)),
            pltpu.SemaphoreType.DMA((2, 6)),
        ],
        compiler_params=pltpu.CompilerParams(vmem_limit_bytes=VMEM_LIMIT),
        cost_estimate=pl.CostEstimate(
            flops=8 * assumed * HD, bytes_accessed=items * 4 * 1024 * 1024, transcendentals=assumed
        ),
    )(me, tables, *[array for array, _ in q_items], pool)
    return result if copy_pool else result[0]


def merge_kernel(a_ref, b_ref, out_ref):
    new_count = a_ref.shape[0]
    lanes = lax.broadcasted_iota(jnp.int32, (new_count, EXTRA), 1)
    terms = jnp.zeros((new_count, EXTRA), jnp.float32)
    for head in range(GROUP):
        stat_a, stat_b = joined_stats(a_ref, head), joined_stats(b_ref, head)
        top = jnp.maximum(stat_a, stat_b)
        share_a, share_b = jnp.exp2(stat_a - top), jnp.exp2(stat_b - top)
        total = share_a + share_b
        columns = pl.ds(head * HD, HD)
        mixed = (
            a_ref[:, columns].astype(jnp.float32) * share_a
            + b_ref[:, columns].astype(jnp.float32) * share_b
        ) / total
        out_ref[:, columns] = mixed.astype(jnp.bfloat16)
        terms = terms + split_stats(top + jnp.log2(total), head, lanes)
    out_ref[:, pl.ds(BLOCK, EXTRA)] = terms.astype(jnp.bfloat16)


def merge(a, b):
    return pl.pallas_call(
        merge_kernel,
        out_shape=jax.ShapeDtypeStruct(a.shape, a.dtype),
        compiler_params=pltpu.CompilerParams(vmem_limit_bytes=VMEM_LIMIT),
        cost_estimate=pl.CostEstimate(
            flops=16 * a.size, bytes_accessed=6 * a.size, transcendentals=2 * a.size
        ),
    )(a, b)


def project_kernel(shards, holders, place_ref, cos_ref, sin_ref, gain_ref, *refs):
    own_ref = refs[0]
    right = refs[1:shards]
    left = refs[shards : 2 * shards - 1]
    weights = refs[2 * shards - 1 : 2 * shards - 1 + 2 * holders]
    out_ref, features, gathered, feature_sem, weight_sem = refs[2 * shards - 1 + 2 * holders :]
    rank, me, group = place_ref[0], place_ref[1], place_ref[2]
    depth = weights[0].shape[0]

    def weight_copies(step):
        owner = me ^ step
        return [
            pltpu.make_async_copy(
                weights[2 * step + kind],
                gathered.at[kind, pl.ds(owner * depth, depth)],
                weight_sem.at[kind, step],
            )
            for kind in range(2)
        ]

    copies = [copy for step in range(holders) for copy in weight_copies(step)]
    for copy in copies:
        copy.start()
    pltpu.make_async_copy(own_ref, features.at[rank], feature_sem.at[0]).start()
    for step in range(1, shards):

        @pl.when(rank >= step)
        def _(step=step):
            pltpu.make_async_copy(
                right[step - 1], features.at[rank - step], feature_sem.at[step]
            ).start()

        @pl.when(rank < step)
        def _(step=step):
            pltpu.make_async_copy(
                left[shards - step - 1], features.at[rank + shards - step], feature_sem.at[step]
            ).start()

    for step in range(shards):
        pltpu.make_async_copy(own_ref, features.at[rank], feature_sem.at[step]).wait()
    for copy in copies:
        copy.wait()
    span = features.shape[2]
    raw = [
        sum(
            plain_dot(features[shard], gathered[kind, pl.ds(shard * span, span)])
            for shard in range(shards)
        )
        for kind in range(2)
    ]
    first = group == 0
    raw_keys = jnp.where(first, raw[0], raw[1])
    raw_values = jnp.where(first, raw[1], raw[0])
    columns = []
    for head in range(raw_keys.shape[1] // HD):
        one = raw_keys[:, head * HD : (head + 1) * HD]
        mean = jnp.sum(one * one, axis=1, keepdims=True) * (1.0 / HD)
        one = one * lax.rsqrt(mean + 1e-06) * gain_ref[...]
        columns.append(one * cos_ref[...] + pltpu.roll(one, HD // 2, 1) * sin_ref[...])
    new_keys = jnp.concatenate(columns, axis=1) if len(columns) > 1 else columns[0]
    out_ref[0] = new_keys.astype(jnp.bfloat16)
    out_ref[1] = raw_values.astype(jnp.bfloat16)


def project(place, cos, sin, gain, own, right, left, weights):
    shards, holders = len(right) + 1, len(weights) // 2
    new_count, span = own.shape
    depth, width = weights[0].shape
    vmem = pl.BlockSpec(memory_space=pltpu.VMEM)
    total = shards * span
    return pl.pallas_call(
        functools.partial(project_kernel, shards, holders),
        out_shape=jax.ShapeDtypeStruct((2, new_count, width), jnp.bfloat16),
        in_specs=[SMEM, vmem, vmem, vmem] + [ANY] * (2 * shards - 1 + 2 * holders),
        out_specs=vmem,
        scratch_shapes=[
            pltpu.VMEM((shards, new_count, span), jnp.bfloat16),
            pltpu.VMEM((2, holders * depth, width), jnp.bfloat16),
            pltpu.SemaphoreType.DMA((shards,)),
            pltpu.SemaphoreType.DMA((2, holders)),
        ],
        compiler_params=pltpu.CompilerParams(vmem_limit_bytes=VMEM_LIMIT),
        cost_estimate=pl.CostEstimate(
            flops=4 * new_count * total * width,
            bytes_accessed=2 * total * (new_count + 2 * width),
            transcendentals=0,
        ),
    )(place, cos, sin, gain, own, *right, *left, *weights)


def final_kernel(kv_local, parts, q_ref, fresh_ref, *refs):
    out_ref = refs[-1]
    new_count = q_ref.shape[0]
    row = lax.broadcasted_iota(jnp.int32, (new_count, new_count), 0)
    column = lax.broadcasted_iota(jnp.int32, (new_count, new_count), 1)
    causal = column <= row
    for kv_head in range(kv_local):
        span = slice(kv_head * HD, (kv_head + 1) * HD)
        keys, values = fresh_ref[0, :, span], fresh_ref[1, :, span]
        partials = refs[kv_head * parts : (kv_head + 1) * parts]
        for head in range(GROUP):
            columns = pl.ds((kv_head * GROUP + head) * HD, HD)
            here = pl.ds(head * HD, HD)
            scores = jnp.where(causal, row_dot(q_ref[:, columns], keys) * SCALE, EMPTY)
            stats = [joined_stats(partial, head) for partial in partials]
            top = jnp.max(scores, axis=1, keepdims=True)
            for stat in stats:
                top = jnp.maximum(top, stat)
            probabilities = [
                jnp.exp2(scores[:, start : start + HD] - top) for start in range(0, new_count, HD)
            ]
            total = jnp.sum(sum(probabilities), axis=1, keepdims=True)
            weights = jnp.concatenate(probabilities, axis=1).astype(jnp.bfloat16)
            mixed = plain_dot(weights, values)
            for stat, partial in zip(stats, partials):
                share = jnp.exp2(stat - top)
                total = total + share
                mixed = mixed + share * partial[:, here].astype(jnp.float32)
            out_ref[:, columns] = (mixed / total).astype(jnp.bfloat16)


def final(queries, fresh, partials):
    kv_local, parts = len(partials), len(partials[0])
    flat = [array for group in partials for array in group]
    size = queries.size
    return pl.pallas_call(
        functools.partial(final_kernel, kv_local, parts),
        out_shape=jax.ShapeDtypeStruct(queries.shape, queries.dtype),
        compiler_params=pltpu.CompilerParams(vmem_limit_bytes=VMEM_LIMIT),
        cost_estimate=pl.CostEstimate(
            flops=4 * size * queries.shape[0],
            bytes_accessed=2 * size * (parts + 2),
            transcendentals=4 * size,
        ),
    )(queries, fresh, *flat)


def write_kernel(holders, new_pages, base, me_ref, table_ref, *refs):
    pages = refs[:holders]
    out_ref, sem = refs[holders + 1], refs[holders + 2]
    me = me_ref[0]

    def each(action):
        for holder in range(holders):
            for page in range(new_pages):

                @pl.when(table_ref[holder, base + page] == me)
                def _(holder=holder, page=page):
                    slot = table_ref[holder, base + new_pages + page]
                    copy = pltpu.make_async_copy(
                        pages[holder].at[:, pl.ds(page * PAGE, PAGE)],
                        out_ref.at[:, slot],
                        sem.at[holder, page],
                    )
                    getattr(copy, action)()

    each("start")
    each("wait")


def write(me, tables, fresh, pool, new_pages, base):
    holders = len(fresh)
    return pl.pallas_call(
        functools.partial(write_kernel, holders, new_pages, base),
        out_shape=jax.ShapeDtypeStruct(pool.shape, pool.dtype),
        in_specs=[SMEM, SMEM] + [ANY] * (holders + 1),
        out_specs=ANY,
        input_output_aliases={2 + holders: 0},
        scratch_shapes=[pltpu.SemaphoreType.DMA((holders, new_pages))],
        compiler_params=pltpu.CompilerParams(vmem_limit_bytes=VMEM_LIMIT),
        cost_estimate=pl.CostEstimate(flops=0, bytes_accessed=4 * fresh[0].size, transcendentals=0),
    )(me, tables, *fresh, pool)


def per_device(
    hidden,
    k_weight,
    v_weight,
    k_gain,
    queries,
    kv_pool,
    page_holder,
    page_slot,
    page_count,
    write_owner,
    write_slot,
):
    inst_count = lax.axis_size("inst")
    shards = lax.axis_size("tp")
    groups = lax.axis_size("groups")
    me = lax.axis_index("inst").astype(jnp.int32)
    rank = lax.axis_index("tp").astype(jnp.int32)
    group = lax.axis_index("groups").astype(jnp.int32)
    pages_listed = page_holder.shape[1]
    new_pages = write_owner.shape[1]
    capacity = 3 * pages_listed // (2 * inst_count)
    new_count = hidden.shape[0]
    kv_local = k_weight.shape[1] // HD
    me_list = me.reshape(1)

    def swap(array, step):
        return lax.ppermute(array, "inst", [(i, i ^ step) for i in range(inst_count)])

    def shift(array, step):
        pairs = [(i, i + step) for i in range(shards) if 0 <= i + step < shards]
        return lax.ppermute(array, "tp", pairs)

    base = 2 * pages_listed + 1
    own_table = jnp.concatenate(
        [page_holder[0], page_slot[0], page_count, write_owner[0], write_slot[0]]
    )
    own_table = jnp.pad(own_table, (0, 128 - own_table.shape[0]))
    table_rows = jnp.pad(
        own_table.astype(jnp.bfloat16)[None, :], ((0, TABLE_ROWS - 1), (0, BLOCK - 128))
    )

    def table_of(payload):
        return payload[new_count, :128].astype(jnp.int32)

    packed = [
        jnp.concatenate([queries[:, k * BLOCK : (k + 1) * BLOCK], table_rows], axis=0)
        for k in range(kv_local)
    ]
    heads = list(range(kv_local))

    asked = {0: packed, 1: [swap(one, 1) for one in packed]}
    for step in range(2, inst_count, 2):
        asked[step] = [swap(one, step) for one in packed]
        asked[step + 1] = [swap(one, 1) for one in asked[step]]
    tables = {0: own_table}
    for step in range(1, inst_count):
        tables[step] = table_of(asked[step][0])

    right, left = [], []
    to_right = to_left = hidden
    for step in range(1, shards):
        to_right, to_left = shift(to_right, 1), shift(to_left, -1)
        right.append(to_right)
        left.append(to_left)

    first = jnp.where(group == 0, k_weight, v_weight)
    second = jnp.where(group == 0, v_weight, k_weight)
    pieces = {0: (first, second), 1: (swap(first, 1), swap(second, 1))}
    for step in range(2, inst_count, 2):
        carried = swap(first, step)
        if groups == 2:
            other = lax.ppermute(carried, "groups", [(0, 1), (1, 0)])
        else:
            other = swap(second, step)
        pieces[step] = (carried, other)
        pieces[step + 1] = (swap(carried, 1), swap(other, 1))
    weights = [piece for step in range(inst_count) for piece in pieces[step]]

    common = dict(
        pool=kv_pool, pages_listed=pages_listed, capacity=capacity, new_count=new_count
    )
    own_part, pool_copy = attend(
        me_list, own_table[None], [(queries, k * BLOCK) for k in heads], heads, copy_pool=True,
        **common,
    )
    mate_part = attend(me_list, tables[1][None], [(one, 0) for one in asked[1]], heads, **common)
    from_mate = swap(mate_part, 1)
    partials = [[own_part[k], from_mate[k]] for k in heads]
    for step in range(2, inst_count, 2):
        pair = jnp.stack([tables[step + 1], tables[step]])
        for k in heads:
            both = attend(
                me_list, pair, [(asked[step + 1][k], 0), (asked[step][k], 0)], [k], **common
            )
            merged = merge(both[1], swap(both[0], 1))
            partials[k].append(swap(merged, step))

    frequency = 1000000.0 ** (-(jnp.arange(HD // 2, dtype=jnp.float32) * 2.0) / HD)
    positions = page_count[0] * PAGE + jnp.arange(new_count, dtype=jnp.int32)
    angles = positions.astype(jnp.float32)[:, None] * frequency[None, :]
    cosine, sine = jnp.cos(angles), jnp.sin(angles)
    fresh = project(
        jnp.stack([rank, me, group]),
        jnp.concatenate([cosine, cosine], axis=1),
        jnp.concatenate([-sine, sine], axis=1),
        k_gain[None, :],
        hidden,
        right,
        left,
        weights,
    )
    attention_out = final(queries, fresh, partials)
    pages = {0: fresh, 1: swap(fresh, 1)}
    for step in range(2, inst_count, 2):
        pages[step] = swap(fresh, step)
        pages[step + 1] = swap(pages[step], 1)
    new_pool = write(
        me_list,
        jnp.stack([tables[step] for step in range(inst_count)]),
        [pages[step] for step in range(inst_count)],
        pool_copy,
        new_pages,
        base,
    )
    return (attention_out, new_pool)


def solution(mesh):
    return jax.shard_map(
        per_device,
        mesh=mesh,
        in_specs=(
            P(("groups", "inst"), "tp"),
            P("inst", "tp"),
            P("inst", "tp"),
            P(),
            P(("groups", "inst"), "tp"),
            P(None, ("groups", "inst"), None, "tp"),
            P(("groups", "inst"), None),
            P(("groups", "inst"), None),
            P(("groups", "inst")),
            P(("groups", "inst"), None),
            P(("groups", "inst"), None),
        ),
        out_specs=(P(("groups", "inst"), "tp"), P(None, ("groups", "inst"), None, "tp")),
        check_vma=False,
    )
```

time: 464 us -> 411 us (0.89)
  the two profiles are of different devices: /device:TPU:5 before, /device:TPU:0 now
where the time goes in v1:
time: 411 us; the launch traced here: 405 us
  Pallas kernels  315 us (77%)
  starting transfers between devices  47.5 us (12%)
  waiting for transfers between devices  20.8 us (5%)
  local copies, waits for them, and re-layouts  13 us (3%)
  other arithmetic  6.7 us (2%)
    pallas_call x4, Pallas kernels, attend(): pl.pallas_call(kernel, out_shape=out_shape, in_specs=[SMEM, SMEM] + [ANY]...  285 us
    ppermute x19, starting transfers between devices, swap(): lax.ppermute(array, 'inst', [(i, i ^ step) for i in range(inst_count)])  28.2 us
    ppermute x19, waiting for transfers between devices, swap(): lax.ppermute(array, 'inst', [(i, i ^ step) for i in range(inst_count)])  20.7 us
    ppermute x6, starting transfers between devices, shift(): return lax.ppermute(array, 'tp', pairs)  17.7 us
    pallas_call x1, Pallas kernels, write(): pl.pallas_call(functools.partial(write_kernel, holders, new_pages, base),...  9.81 us
  transfers between devices with their start and end apart: 26, of which 2 were waited for; matrix products, arithmetic and copies ran while one was open for 3% of the time, Pallas kernels for 75%

profile of v1, /device:TPU:0, one launch (start us, length us, event | category | flops | bytes accessed | tf_op | source)
XLA Modules:
  0.0 405.5 jit_solution(10331801600915706346)
XLA Ops:
  2.6 1.3 fusion.4
  3.9 0.9 fusion.2
  4.8 2.9 collective-permute-start.19
  8.3 3.8 collective-permute-start
  13.5 0.8 pad_maximum_fusion
  14.3 217.9 %shard_map.123 = (bf16[2,256,1152]{2,1,0:T(8,128)(2,1)}, bf16[2,54,128,256]{3,2,1,0:T(8,128)(2,1)}) custom-call(s32[1]{0:T(128)} %bitcast.1.me_ref, s32[1,128]{1,0:T(1,128)} %get-tuple-element.24.table_ref, bf16[256,2048]{1,0:T(8,128)(2,1)} %q_ref.1, bf16[256,2048]{1,0:T(8,128)(2,1)} %q_ref.1, bf16[2,54,128,256]{3,2,1,0:T(8,128)(2,1)} %refs_2_.7), custom_call_target="tpu_custom_call" | custom-call | flops 4294967296 | bytes 8388608 | tf_op jit(solution)/shard_map/pallas_call | solution.py:229
  232.3 1.8 collective-permute-start.3
  234.1 1.2 slice_convert_fusion.2.table_ref
  235.3 1.5 collective-permute-start.8
  237.3 12.6 %shard_map.124 = bf16[2,256,1152]{2,1,0:T(8,128)(2,1)} custom-call(s32[1]{0:T(128)} %bitcast.1.me_ref, s32[1,128]{1,0:T(1,128)} %slice_convert_fusion.2.table_ref, bf16[272,1024]{1,0:T(8,128)(2,1)} %collective-permute-done.12.refs_0_, bf16[272,1024]{1,0:T(8,128)(2,1)} %collective-permute-done.13.refs_1_, bf16[2,54,128,256]{3,2,1,0:T(8,128)(2,1)} %refs_2_.7), custom_call_target="tpu_custom_call" | custom-call | flops 4294967296 | bytes 8388608 | tf_op jit(solution)/shard_map/pallas_call | solution.py:229
  250.7 19.0 %collective-permute-start.6 = (bf16[1280,256]{1,0:T(8,128)(2,1)S(1)}, bf16[1280,256]{1,0:T(8,128)(2,1)S(1)}, u32[]{:S(2)}, u32[]{:S(2)}) collective-permute-start(bf16[1280,256]{1,0:T(8,128)(2,1)S(1)} %get-tuple-element.7.refs_7_), channel_id=1, source_target_pairs={{0,4},{4,0},{8,12},{12,8},{1,5},{5,1},{9,13},{13,9},{2,6},{6,2},{1... | collective-permute-start | bytes 1966088 | tf_op jit(solution)/shard_map/ppermute | solution.py:486
  270.4 4.6 %collective-permute-start.1 = (bf16[256,1280]{1,0:T(8,128)(2,1)S(1)}, bf16[256,1280]{1,0:T(8,128)(2,1)S(1)}, u32[]{:S(2)}, u32[]{:S(2)}) collective-permute-start(bf16[256,1280]{1,0:T(8,128)(2,1)S(1)} %collective-permute-done.refs_1_), channel_id=1, source_target_pairs={{0,1},{1,2},{2,3},{4,5},{5,6},{6,7},{8,9},{9,10},{10,11},{12,13},{... | collective-permute-start | bytes 1966088 | tf_op jit(solution)/shard_map/ppermute | solution.py:490
  275.0 1.5 collective-permute-start.4
  276.5 1.6 collective-permute-start.9
  278.1 27.1 %shard_map.127 = bf16[2,256,1152]{2,1,0:T(8,128)(2,1)} custom-call(s32[1]{0:T(128)} %bitcast.1.me_ref, s32[2,128]{1,0:T(2,128)} %pad_add_fusion.1.table_ref, bf16[272,1024]{1,0:T(8,128)(2,1)} %copy-done.28, bf16[272,1024]{1,0:T(8,128)(2,1)} %collective-permute-done.19.refs_1_, bf16[2,54,128,256]{3,2,1,0:T(8,128)(2,1)} %refs_2_.7), custom_call_target="tpu_custom_call" | custom-call | flops 4294967296 | bytes 8388608 | tf_op jit(solution)/shard_map/pallas_call | solution.py:229
  305.2 2.2 slice_bitcast_fusion
  307.5 4.6 %collective-permute-start.2 = (bf16[256,1280]{1,0:T(8,128)(2,1)S(1)}, bf16[256,1280]{1,0:T(8,128)(2,1)S(1)}, u32[]{:S(2)}, u32[]{:S(2)}) collective-permute-start(bf16[256,1280]{1,0:T(8,128)(2,1)S(1)} %collective-permute-done.1.refs_2_), channel_id=1, source_target_pairs={{0,1},{1,2},{2,3},{4,5},{5,6},{6,7},{8,9},{9,10},{10,11},{12,13},{... | collective-permute-start | bytes 1966088 | tf_op jit(solution)/shard_map/ppermute | solution.py:490
  312.1 1.5 collective-permute-start.5
  313.9 27.0 %shard_map.125 = bf16[2,256,1152]{2,1,0:T(8,128)(2,1)} custom-call(s32[1]{0:T(128)} %bitcast.1.me_ref, s32[2,128]{1,0:T(2,128)} %pad_add_fusion.1.table_ref, bf16[272,1024]{1,0:T(8,128)(2,1)} %copy-done.27, bf16[272,1024]{1,0:T(8,128)(2,1)} %collective-permute-done.15.refs_1_, bf16[2,54,128,256]{3,2,1,0:T(8,128)(2,1)} %refs_2_.7), custom_call_target="tpu_custom_call" | custom-call | flops 4294967296 | bytes 8388608 | tf_op jit(solution)/shard_map/pallas_call | solution.py:229
  341.0 2.4 slice_bitcast_fusion.3
  344.9 6.8 %shard_map.122.fresh_ref.refs_0_ = bf16[2,256,256]{2,1,0:T(8,128)(2,1)} custom-call(s32[3]{0:T(128)} %pad_add_fusion.2.place_ref, f32[256,128]{1,0:T(8,128)} %get-tuple-element.25.cos_ref, f32[256,128]{1,0:T(8,128)} %get-tuple-element.26.sin_ref, f32[1,128]{1,0:T(1,128)} %bitcast.29, bf16[256,1280]{1,0:T(8,128)(2,1)} %refs_0_.2, ...), custom_call_target="tpu_custom_call" | custom-call | flops 1342177280 | bytes 7864320 | tf_op jit(solution)/shard_map/pallas_call | solution.py:355
  351.8 1.1 slice_bitcast_fusion.6
  352.9 0.8 copy-done.21
  353.7 3.1 shard_map.126
  356.8 2.0 collective-permute-start.18
  358.8 0.8 copy-done.20
  359.6 3.1 shard_map.128
  363.9 1.2 slice_bitcast_fusion.2
  365.0 8.6 %collective-permute-done.18.refs_2_ = bf16[256,1152]{1,0:T(8,128)(2,1)S(1)} collective-permute-done((bf16[256,1152]{1,0:T(8,128)(2,1)}, bf16[256,1152]{1,0:T(8,128)(2,1)S(1)}, u32[]{:S(2)}, u32[]{:S(2)}) %collective-permute-start.18) | collective-permute-done | bytes 589856 | tf_op jit(solution)/shard_map/ppermute | solution.py:486
  373.6 12.2 %collective-permute-done.22.refs_5_ = bf16[256,1152]{1,0:T(8,128)(2,1)S(1)} collective-permute-done((bf16[256,1152]{1,0:T(8,128)(2,1)}, bf16[256,1152]{1,0:T(8,128)(2,1)S(1)}, u32[]{:S(2)}, u32[]{:S(2)}) %collective-permute-start.22) | collective-permute-done | bytes 589856 | tf_op jit(solution)/shard_map/ppermute | solution.py:486
  386.6 8.0 %shard_map.129 = bf16[256,2048]{1,0:T(8,128)(2,1)} custom-call(bf16[256,2048]{1,0:T(8,128)(2,1)} %q_ref.1, bf16[2,256,256]{2,1,0:T(8,128)(2,1)} %shard_map.122.fresh_ref.refs_0_, bf16[256,1152]{1,0:T(8,128)(2,1)} %get-tuple-element.13.refs_0_, bf16[256,1152]{1,0:T(8,128)(2,1)} %get-tuple-element.11.refs_1_, bf16[256,1152]{1,0:T(8,128)(2,1)} %copy-done.18, ...), custom_call_target="tpu_custom_call" | custom-call | flops 536870912 | bytes 5242880 | tf_op jit(solution)/shard_map/pallas_call | solution.py:410
  395.4 9.8 %shard_map.130 = bf16[2,54,128,256]{3,2,1,0:T(8,128)(2,1)} custom-call(s32[1]{0:T(128)} %bitcast.1.me_ref, s32[4,128]{1,0:T(4,128)} %pad_add_fusion.table_ref, bf16[2,256,256]{2,1,0:T(8,128)(2,1)} %shard_map.122.fresh_ref.refs_0_, bf16[2,256,256]{2,1,0:T(8,128)(2,1)} %copy-done.23, bf16[2,256,256]{2,1,0:T(8,128)(2,1)} %copy-done.22, ...), custom_call_target="tpu_custom_call", output_to_operand_aliasing={{}: (6, {})} | custom-call | bytes 524288 | tf_op jit(solution)/shard_map/pallas_call | solution.py:447
  (106 shorter events, 9.9 us)
Async XLA Ops:
  4.8 230.5 %collective-permute-start.19 = (bf16[272,1024]{1,0:T(8,128)(2,1)}, bf16[272,1024]{1,0:T(8,128)(2,1)}, u32[]{:S(2)}, u32[]{:S(2)}) collective-permute-start(bf16[272,1024]{1,0:T(8,128)(2,1)} %get-tuple-element.21), channel_id=1, source_target_pairs={{0,8},{4,12},{8,0},{12,4},{1,9},{5,13},{9,1},{13,5},{2,10},{6,14},... | collective-permute-start | bytes 1671176 | tf_op jit(solution)/shard_map/ppermute | solution.py:486
  7.8 229.0 %collective-permute-start.13 = (bf16[272,1024]{1,0:T(8,128)(2,1)}, bf16[272,1024]{1,0:T(8,128)(2,1)}, u32[]{:S(2)}, u32[]{:S(2)}) collective-permute-start(bf16[272,1024]{1,0:T(8,128)(2,1)} %get-tuple-element.21), channel_id=1, source_target_pairs={{0,4},{4,0},{8,12},{12,8},{1,5},{5,1},{9,13},{13,9},{2,6},{6,2},{1... | collective-permute-start | bytes 1671176 | tf_op jit(solution)/shard_map/ppermute | solution.py:486
  7.8 229.1 %collective-permute-start.15 = (bf16[272,1024]{1,0:T(8,128)(2,1)S(1)}, bf16[272,1024]{1,0:T(8,128)(2,1)}, u32[]{:S(2)}, u32[]{:S(2)}) collective-permute-start(bf16[272,1024]{1,0:T(8,128)(2,1)S(1)} %get-tuple-element.22), channel_id=1, source_target_pairs={{0,8},{4,12},{8,0},{12,4},{1,9},{5,13},{9,1},{13,5},{2,10},{6,14},... | collective-permute-start | bytes 1671176 | tf_op jit(solution)/shard_map/ppermute | solution.py:486
  7.8 224.5 %collective-permute-start.12 = (bf16[272,1024]{1,0:T(8,128)(2,1)S(1)}, bf16[272,1024]{1,0:T(8,128)(2,1)}, u32[]{:S(2)}, u32[]{:S(2)}) collective-permute-start(bf16[272,1024]{1,0:T(8,128)(2,1)S(1)} %get-tuple-element.22), channel_id=1, source_target_pairs={{0,4},{4,0},{8,12},{12,8},{1,5},{5,1},{9,13},{13,9},{2,6},{6,2},{1... | collective-permute-start | bytes 1671176 | tf_op jit(solution)/shard_map/ppermute | solution.py:486
  8.3 261.9 %collective-permute-start = (bf16[256,1280]{1,0:T(8,128)(2,1)S(1)}, bf16[256,1280]{1,0:T(8,128)(2,1)S(1)}, u32[]{:S(2)}, u32[]{:S(2)}) collective-permute-start(bf16[256,1280]{1,0:T(8,128)(2,1)S(1)} %copy-done.6), channel_id=1, source_target_pairs={{0,1},{1,2},{2,3},{4,5},{5,6},{6,7},{8,9},{9,10},{10,11},{12,13},{... | collective-permute-start | bytes 1966088 | tf_op jit(solution)/shard_map/ppermute | solution.py:490
  12.8 237.9 %copy-start.1 = (bf16[1280,256]{1,0:T(8,128)(2,1)}, bf16[1280,256]{1,0:T(8,128)(2,1)S(1)}, u32[]{:S(2)}) copy-start(bf16[1280,256]{1,0:T(8,128)(2,1)S(1)} %get-tuple-element.7.refs_7_) | copy-start | bytes 1966084
  12.8 257.4 %copy-start = (bf16[1280,256]{1,0:T(8,128)(2,1)}, bf16[1280,256]{1,0:T(8,128)(2,1)S(1)}, u32[]{:S(2)}) copy-start(bf16[1280,256]{1,0:T(8,128)(2,1)S(1)} %get-tuple-element.6.refs_8_) | copy-start | bytes 1966084
  232.3 38.1 %collective-permute-start.3 = (bf16[256,1280]{1,0:T(8,128)(2,1)S(1)}, bf16[256,1280]{1,0:T(8,128)(2,1)S(1)}, u32[]{:S(2)}, u32[]{:S(2)}) collective-permute-start(bf16[256,1280]{1,0:T(8,128)(2,1)S(1)} %copy-done.6), channel_id=1, source_target_pairs={{1,0},{2,1},{3,2},{5,4},{6,5},{7,6},{9,8},{10,9},{11,10},{13,12},{... | collective-permute-start | bytes 1966088 | tf_op jit(solution)/shard_map/ppermute | solution.py:490
  235.3 39.6 %collective-permute-start.8 = (bf16[1280,256]{1,0:T(8,128)(2,1)S(1)}, bf16[1280,256]{1,0:T(8,128)(2,1)S(1)}, u32[]{:S(2)}, u32[]{:S(2)}) collective-permute-start(bf16[1280,256]{1,0:T(8,128)(2,1)S(1)} %get-tuple-element.7.refs_7_), channel_id=1, source_target_pairs={{0,8},{4,12},{8,0},{12,4},{1,9},{5,13},{9,1},{13,5},{2,10},{6,14},... | collective-permute-start | bytes 1966088 | tf_op jit(solution)/shard_map/ppermute | solution.py:486
  236.8 39.6 %collective-permute-start.20 = (bf16[272,1024]{1,0:T(8,128)(2,1)}, bf16[272,1024]{1,0:T(8,128)(2,1)S(1)}, u32[]{:S(2)}, u32[]{:S(2)}) collective-permute-start(bf16[272,1024]{1,0:T(8,128)(2,1)} %collective-permute-done.19.refs_1_), channel_id=1, source_target_pairs={{0,4},{4,0},{8,12},{12,8},{1,5},{5,1},{9,13},{13,9},{2,6},{6,2},{1... | collective-permute-start | bytes 1671176 | tf_op jit(solution)/shard_map/ppermute | solution.py:486
  236.8 13.8 %collective-permute-start.16 = (bf16[272,1024]{1,0:T(8,128)(2,1)}, bf16[272,1024]{1,0:T(8,128)(2,1)S(1)}, u32[]{:S(2)}, u32[]{:S(2)}) collective-permute-start(bf16[272,1024]{1,0:T(8,128)(2,1)} %collective-permute-done.15.refs_1_), channel_id=1, source_target_pairs={{0,4},{4,0},{8,12},{12,8},{1,5},{5,1},{9,13},{13,9},{2,6},{6,2},{1... | collective-permute-start | bytes 1671176 | tf_op jit(solution)/shard_map/ppermute | solution.py:486
  250.7 90.3 %collective-permute-start.6 = (bf16[1280,256]{1,0:T(8,128)(2,1)S(1)}, bf16[1280,256]{1,0:T(8,128)(2,1)S(1)}, u32[]{:S(2)}, u32[]{:S(2)}) collective-permute-start(bf16[1280,256]{1,0:T(8,128)(2,1)S(1)} %get-tuple-element.7.refs_7_), channel_id=1, source_target_pairs={{0,4},{4,0},{8,12},{12,8},{1,5},{5,1},{9,13},{13,9},{2,6},{6,2},{1... | collective-permute-start | bytes 1966088 | tf_op jit(solution)/shard_map/ppermute | solution.py:486
  270.2 35.0 %copy-start.7 = (bf16[256,1280]{1,0:T(8,128)(2,1)}, bf16[256,1280]{1,0:T(8,128)(2,1)S(1)}, u32[]{:S(2)}) copy-start(bf16[256,1280]{1,0:T(8,128)(2,1)S(1)} %collective-permute-done.refs_1_) | copy-start | bytes 1966084
  270.2 37.1 %collective-permute-start.7 = (bf16[1280,256]{1,0:T(8,128)(2,1)S(1)}, bf16[1280,256]{1,0:T(8,128)(2,1)S(1)}, u32[]{:S(2)}, u32[]{:S(2)}) collective-permute-start(bf16[1280,256]{1,0:T(8,128)(2,1)S(1)} %get-tuple-element.6.refs_8_), channel_id=1, source_target_pairs={{0,4},{4,0},{8,12},{12,8},{1,5},{5,1},{9,13},{13,9},{2,6},{6,2},{1... | collective-permute-start | bytes 1966088 | tf_op jit(solution)/shard_map/ppermute | solution.py:486
  270.4 34.8 %copy-start.8 = (bf16[256,1280]{1,0:T(8,128)(2,1)}, bf16[256,1280]{1,0:T(8,128)(2,1)S(1)}, u32[]{:S(2)}) copy-start(bf16[256,1280]{1,0:T(8,128)(2,1)S(1)} %collective-permute-done.3.refs_4_) | copy-start | bytes 1966084
  270.4 37.1 %collective-permute-start.1 = (bf16[256,1280]{1,0:T(8,128)(2,1)S(1)}, bf16[256,1280]{1,0:T(8,128)(2,1)S(1)}, u32[]{:S(2)}, u32[]{:S(2)}) collective-permute-start(bf16[256,1280]{1,0:T(8,128)(2,1)S(1)} %collective-permute-done.refs_1_), channel_id=1, source_target_pairs={{0,1},{1,2},{2,3},{4,5},{5,6},{6,7},{8,9},{9,10},{10,11},{12,13},{... | collective-permute-start | bytes 1966088 | tf_op jit(solution)/shard_map/ppermute | solution.py:490
  275.0 37.1 %collective-permute-start.4 = (bf16[256,1280]{1,0:T(8,128)(2,1)S(1)}, bf16[256,1280]{1,0:T(8,128)(2,1)S(1)}, u32[]{:S(2)}, u32[]{:S(2)}) collective-permute-start(bf16[256,1280]{1,0:T(8,128)(2,1)S(1)} %collective-permute-done.3.refs_4_), channel_id=1, source_target_pairs={{1,0},{2,1},{3,2},{5,4},{6,5},{7,6},{9,8},{10,9},{11,10},{13,12},{... | collective-permute-start | bytes 1966088 | tf_op jit(solution)/shard_map/ppermute | solution.py:490
  276.5 37.1 %collective-permute-start.9 = (bf16[1280,256]{1,0:T(8,128)(2,1)S(1)}, bf16[1280,256]{1,0:T(8,128)(2,1)S(1)}, u32[]{:S(2)}, u32[]{:S(2)}) collective-permute-start(bf16[1280,256]{1,0:T(8,128)(2,1)S(1)} %collective-permute-done.8.refs_11_), channel_id=1, source_target_pairs={{0,16},{16,0},{1,17},{17,1},{2,18},{18,2},{3,19},{19,3},{4,20},{20... | collective-permute-start | bytes 1966088 | tf_op jit(solution)/shard_map/ppermute | solution.py:531
  307.4 33.5 %copy-start.11 = (bf16[1280,256]{1,0:T(8,128)(2,1)}, bf16[1280,256]{1,0:T(8,128)(2,1)S(1)}, u32[]{:S(2)}) copy-start(bf16[1280,256]{1,0:T(8,128)(2,1)S(1)} %collective-permute-done.7.refs_10_) | copy-start | bytes 1966084
  307.4 36.0 %collective-permute-start.10 = (bf16[1280,256]{1,0:T(8,128)(2,1)S(1)}, bf16[1280,256]{1,0:T(8,128)(2,1)S(1)}, u32[]{:S(2)}, u32[]{:S(2)}) collective-permute-start(bf16[1280,256]{1,0:T(8,128)(2,1)S(1)} %collective-permute-done.8.refs_11_), channel_id=1, source_target_pairs={{0,4},{4,0},{8,12},{12,8},{1,5},{5,1},{9,13},{13,9},{2,6},{6,2},{1... | collective-permute-start | bytes 1966088 | tf_op jit(solution)/shard_map/ppermute | solution.py:486
  307.5 33.4 %copy-start.12 = (bf16[256,1280]{1,0:T(8,128)(2,1)}, bf16[256,1280]{1,0:T(8,128)(2,1)S(1)}, u32[]{:S(2)}) copy-start(bf16[256,1280]{1,0:T(8,128)(2,1)S(1)} %collective-permute-done.1.refs_2_) | copy-start | bytes 1966084
  307.5 36.3 %collective-permute-start.2 = (bf16[256,1280]{1,0:T(8,128)(2,1)S(1)}, bf16[256,1280]{1,0:T(8,128)(2,1)S(1)}, u32[]{:S(2)}, u32[]{:S(2)}) collective-permute-start(bf16[256,1280]{1,0:T(8,128)(2,1)S(1)} %collective-permute-done.1.refs_2_), channel_id=1, source_target_pairs={{0,1},{1,2},{2,3},{4,5},{5,6},{6,7},{8,9},{9,10},{10,11},{12,13},{... | collective-permute-start | bytes 1966088 | tf_op jit(solution)/shard_map/ppermute | solution.py:490
  312.1 31.9 %collective-permute-start.5 = (bf16[256,1280]{1,0:T(8,128)(2,1)S(1)}, bf16[256,1280]{1,0:T(8,128)(2,1)S(1)}, u32[]{:S(2)}, u32[]{:S(2)}) collective-permute-start(bf16[256,1280]{1,0:T(8,128)(2,1)S(1)} %collective-permute-done.4.refs_5_), channel_id=1, source_target_pairs={{1,0},{2,1},{3,2},{5,4},{6,5},{7,6},{9,8},{10,9},{11,10},{13,12},{... | collective-permute-start | bytes 1966088 | tf_op jit(solution)/shard_map/ppermute | solution.py:490
  313.6 30.4 %collective-permute-start.11 = (bf16[1280,256]{1,0:T(8,128)(2,1)S(1)}, bf16[1280,256]{1,0:T(8,128)(2,1)}, u32[]{:S(2)}, u32[]{:S(2)}) collective-permute-start(bf16[1280,256]{1,0:T(8,128)(2,1)S(1)} %collective-permute-done.9.refs_12_), channel_id=1, source_target_pairs={{0,4},{4,0},{8,12},{12,8},{1,5},{5,1},{9,13},{13,9},{2,6},{6,2},{1... | collective-permute-start | bytes 1966088 | tf_op jit(solution)/shard_map/ppermute | solution.py:486
  340.9 22.9 %collective-permute-start.14 = (bf16[2,256,1152]{2,1,0:T(8,128)(2,1)}, bf16[2,256,1152]{2,1,0:T(8,128)(2,1)S(1)}, u32[]{:S(2)}, u32[]{:S(2)}) collective-permute-start(bf16[2,256,1152]{2,1,0:T(8,128)(2,1)} %shard_map.124), channel_id=1, source_target_pairs={{0,4},{4,0},{8,12},{12,8},{1,5},{5,1},{9,13},{13,9},{2,6},{6,2},{1... | collective-permute-start | bytes 3538952 | tf_op jit(solution)/shard_map/ppermute | solution.py:486
  343.4 9.5 %collective-permute-start.17 = (bf16[256,1152]{1,0:T(8,128)(2,1)S(1)}, bf16[256,1152]{1,0:T(8,128)(2,1)S(1)}, u32[]{:S(2)}, u32[]{:S(2)}) collective-permute-start(bf16[256,1152]{1,0:T(8,128)(2,1)S(1)} %get-tuple-element.14), channel_id=1, source_target_pairs={{0,4},{4,0},{8,12},{12,8},{1,5},{5,1},{9,13},{13,9},{2,6},{6,2},{1... | collective-permute-start | bytes 1769480 | tf_op jit(solution)/shard_map/ppermute | solution.py:486
  343.8 15.0 %collective-permute-start.21 = (bf16[256,1152]{1,0:T(8,128)(2,1)S(1)}, bf16[256,1152]{1,0:T(8,128)(2,1)S(1)}, u32[]{:S(2)}, u32[]{:S(2)}) collective-permute-start(bf16[256,1152]{1,0:T(8,128)(2,1)S(1)} %get-tuple-element.8), channel_id=1, source_target_pairs={{0,4},{4,0},{8,12},{12,8},{1,5},{5,1},{9,13},{13,9},{2,6},{6,2},{1... | collective-permute-start | bytes 1769480 | tf_op jit(solution)/shard_map/ppermute | solution.py:486
  351.7 11.7 %collective-permute-start.24 = (bf16[2,256,256]{2,1,0:T(8,128)(2,1)}, bf16[2,256,256]{2,1,0:T(8,128)(2,1)S(1)}, u32[]{:S(2)}, u32[]{:S(2)}) collective-permute-start(bf16[2,256,256]{2,1,0:T(8,128)(2,1)} %shard_map.122.fresh_ref.refs_0_), channel_id=1, source_target_pairs={{0,8},{4,12},{8,0},{12,4},{1,9},{5,13},{9,1},{13,5},{2,10},{6,14},... | collective-permute-start | bytes 786440 | tf_op jit(solution)/shard_map/ppermute | solution.py:486
  356.8 16.8 %collective-permute-start.18 = (bf16[256,1152]{1,0:T(8,128)(2,1)}, bf16[256,1152]{1,0:T(8,128)(2,1)S(1)}, u32[]{:S(2)}, u32[]{:S(2)}) collective-permute-start(bf16[256,1152]{1,0:T(8,128)(2,1)} %shard_map.126), channel_id=1, source_target_pairs={{0,8},{4,12},{8,0},{12,4},{1,9},{5,13},{9,1},{13,5},{2,10},{6,14},... | collective-permute-start | bytes 1769480 | tf_op jit(solution)/shard_map/ppermute | solution.py:486
  362.7 23.0 %collective-permute-start.22 = (bf16[256,1152]{1,0:T(8,128)(2,1)}, bf16[256,1152]{1,0:T(8,128)(2,1)S(1)}, u32[]{:S(2)}, u32[]{:S(2)}) collective-permute-start(bf16[256,1152]{1,0:T(8,128)(2,1)} %shard_map.128), channel_id=1, source_target_pairs={{0,8},{4,12},{8,0},{12,4},{1,9},{5,13},{9,1},{13,5},{2,10},{6,14},... | collective-permute-start | bytes 1769480 | tf_op jit(solution)/shard_map/ppermute | solution.py:486
  363.4 31.2 %collective-permute-start.23 = (bf16[2,256,256]{2,1,0:T(8,128)(2,1)S(1)}, bf16[2,256,256]{2,1,0:T(8,128)(2,1)S(1)}, u32[]{:S(2)}, u32[]{:S(2)}) collective-permute-start(bf16[2,256,256]{2,1,0:T(8,128)(2,1)S(1)} %copy-done.2), channel_id=1, source_target_pairs={{0,4},{4,0},{8,12},{12,8},{1,5},{5,1},{9,13},{13,9},{2,6},{6,2},{1... | collective-permute-start | bytes 786440 | tf_op jit(solution)/shard_map/ppermute | solution.py:486
  363.4 31.2 %collective-permute-start.25 = (bf16[2,256,256]{2,1,0:T(8,128)(2,1)S(1)}, bf16[2,256,256]{2,1,0:T(8,128)(2,1)S(1)}, u32[]{:S(2)}, u32[]{:S(2)}) collective-permute-start(bf16[2,256,256]{2,1,0:T(8,128)(2,1)S(1)} %collective-permute-done.24.refs_2_), channel_id=1, source_target_pairs={{0,4},{4,0},{8,12},{12,8},{1,5},{5,1},{9,13},{13,9},{2,6},{6,2},{1... | collective-permute-start | bytes 786440 | tf_op jit(solution)/shard_map/ppermute | solution.py:486
  (23 other events, 184.5 us)
